TPU v7x, 256 devices: a whole 4x4x8 slice. The times are simulated.
256 devices in a mesh: dp: 64 (over x, y_hi, z), ctx: 4 (over y_lo, core).
Axes of the slice: x: 4, y: 4 (y_hi: 2, y_lo: 2; y = y_hi * 2 + y_lo), z: 8, core: 2. Of those that a mesh axis runs over, the one named last changes fastest.
Arguments:
- frames: bfloat16 [64, 1024, 1536], P('dp', 'ctx'), may hold values from -6 to 6
- destinations: int32 [64, 1024], P('dp', 'ctx'), may hold values from 0 to 16383, as said below
- segments: int32 [64, 1024], P('dp'), may hold values from 0 to 2, as said below
- tile_mask: int32 [64, 8, 8], P('dp', 'ctx'), may hold values from 0 to 1, as said below
- attn_gain: float32 [1536], replicated, may hold values from 0.1 to 1.9
- w_qkv: bfloat16 [1536, 2304], replicated
- w_out: bfloat16 [768, 1536], replicated, may hold values from -5 to 5
- conv_gain: float32 [1536], replicated, may hold values from 0.1 to 1.9
- w_pointin: bfloat16 [1536, 1536], P(('dp', 'ctx')), may hold values from -0.625 to 0.625
- w_pointout: bfloat16 [768, 1536], P(None, ('dp', 'ctx')), may hold values from -0.43164062 to 0.43164062
- w_depth: float32 [32, 768], replicated, may hold values from -1 to 1
- bn_scale: float32 [768], replicated, may hold values from 0.1 to 1.9
- bn_shift: float32 [768], replicated, may hold values from -3 to 3
Outputs:
- layer_out: bfloat16 [64, 1024, 1536], P('dp', 'ctx')
Inputs may be any that keep to these rules, and one draw needn't show every extreme that they name: `destinations`: per ctx index c, the values at positions c * 256 to (c + 1) * 256 - 1 over all rows of the first dimension are all different, so every target row is filled once. The rows of one device send at most 8 frames to one sequence, and exactly 8 to some sequences. `segments`: along a sequence the ids never fall, start at 0 and end at 2. tile_mask[b, t, t] = 1; tile_mask[b, t, u] = 0 where tiles t and u of sequence b share no segment id.
All inputs are finite; a program needn't handle non-finite values.
Results may differ from a plain program's by a relative error of at most 0.01.
Values may be sent and summed in bfloat16 or wider, within the bound.
A program may use at most 128 MiB of HBM per device.

v0:
```python
import math
import jax
import jax.numpy as jnp
from jax import lax
from jax.sharding import PartitionSpec as P

HEADS = 8


def padded_2(cells, sides, width):
    for axis, dim in sides:
        count = lax.axis_size(axis)
        ends = count - 1
        head = lax.slice_in_dim(cells, 0, width, axis=dim)
        tail = lax.slice_in_dim(cells, cells.shape[dim] - width, cells.shape[dim], axis=dim)
        cells = jnp.concatenate(
            [
                lax.ppermute(tail, axis, [(i, (i + 1) % count) for i in range(ends)]),
                cells,
                lax.ppermute(head, axis, [((i + 1) % count, i) for i in range(ends)]),
            ],
            axis=dim,
        )
    return cells


def layer_norm(values, gain):
    as_float = values.astype(jnp.float32)
    row_mean = jnp.mean(as_float, axis=-1, keepdims=True)
    centred = as_float - row_mean
    row_var = jnp.mean(centred * centred, axis=-1, keepdims=True)
    return centred * lax.rsqrt(row_var + 1e-06) * gain


def per_device(
    frames,
    destinations,
    segments,
    tile_mask,
    attn_gain,
    w_qkv,
    w_out,
    conv_gain,
    w_pointin,
    w_pointout,
    w_depth,
    bn_scale,
    bn_shift,
):
    row_count = frames.shape[1]
    width = frames.shape[2]
    peer_count = lax.axis_size("dp")
    capacity = 2 * row_count // peer_count
    own_frames = frames[0]
    targets = destinations[0]
    owner_index = targets // row_count
    slot_index = targets % row_count
    onehot = (owner_index[:, None] == jnp.arange(peer_count, dtype=jnp.int32)[None, :]).astype(
        jnp.int32
    )
    before = jnp.cumsum(onehot, axis=0) - onehot
    rank_in = jnp.sum(before * onehot, axis=1)
    position = owner_index * capacity + rank_in
    send_rows = jnp.zeros((peer_count * capacity, width), jnp.bfloat16).at[position].set(own_frames)
    send_slots = (
        jnp.full((peer_count * capacity,), row_count, jnp.int32).at[position].set(slot_index)
    )
    got_rows, got_slots = (
        lax.all_to_all(
            send_rows.reshape(peer_count, capacity, width),
            "dp",
            split_axis=0,
            concat_axis=0,
            tiled=True,
        ),
        lax.all_to_all(
            send_slots.reshape(peer_count, capacity), "dp", split_axis=0, concat_axis=0, tiled=True
        ),
    )
    placed = (
        jnp.zeros((row_count, width), jnp.bfloat16)
        .at[got_slots.reshape(-1)]
        .set(got_rows.reshape(-1, width), mode="drop")
    )
    shard_start = lax.axis_index("ctx") * row_count
    seg_row = segments[0]
    own_seg = lax.dynamic_slice_in_dim(seg_row, shard_start, row_count, 0)
    mask_rows = tile_mask[0]
    tile_size = row_count // mask_rows.shape[0]
    head_cols = w_out.shape[0]
    head_size = head_cols // HEADS
    scale_factor = 1.0 / math.sqrt(head_size)
    normed = layer_norm(placed, attn_gain).astype(jnp.bfloat16)
    qkv_rows = jnp.dot(normed, w_qkv, preferred_element_type=jnp.float32).astype(jnp.bfloat16)
    queries = qkv_rows[:, :head_cols].reshape(row_count, HEADS, head_size)
    key_rows = qkv_rows[:, head_cols : 2 * head_cols].reshape(row_count, HEADS, head_size)
    value_rows = qkv_rows[:, 2 * head_cols :].reshape(row_count, HEADS, head_size)

    def absorb(carry, block):
        key_block, value_block, seg_block, mask_block = block
        wide_mask = jnp.repeat(jnp.repeat(mask_block, tile_size, axis=0), tile_size, axis=1)
        allowed = (own_seg[:, None] == seg_block[None, :]) & (wide_mask == 1)
        running_max, running_sum, weighted = carry
        scores = (
            jnp.einsum("qhd,khd->hqk", queries, key_block, preferred_element_type=jnp.float32)
            * scale_factor
        )
        scores = jnp.where(allowed[None], scores, -1e30)
        new_max = jnp.maximum(running_max, jnp.max(scores, axis=-1))
        weights = jnp.where(allowed[None], jnp.exp(scores - new_max[:, :, None]), 0.0)
        factor = jnp.exp(running_max - new_max)
        new_sum = running_sum * factor + jnp.sum(weights, axis=-1)
        product = jnp.einsum(
            "hqk,khd->hqd",
            weights.astype(jnp.bfloat16),
            value_block,
            preferred_element_type=jnp.float32,
        )
        return ((new_max, new_sum, weighted * factor[:, :, None] + product), None)

    start_state = (
        jnp.full((HEADS, row_count), -1e30, jnp.float32),
        jnp.zeros((HEADS, row_count), jnp.float32),
        jnp.zeros((HEADS, row_count, head_size), jnp.float32),
    )
    keys_piece = lax.all_gather(key_rows, "ctx", axis=0, tiled=True)
    values_piece = lax.all_gather(value_rows, "ctx", axis=0, tiled=True)
    count = keys_piece.shape[0]
    block_rows = math.gcd(count, 512)
    blocks = count // block_rows
    mask_piece = mask_rows
    mask_piece = jnp.transpose(
        mask_piece.reshape(mask_rows.shape[0], blocks, block_rows // tile_size), (1, 0, 2)
    )
    inputs = (
        keys_piece.reshape(blocks, block_rows, HEADS, head_size),
        values_piece.reshape(blocks, block_rows, HEADS, head_size),
        seg_row.reshape(blocks, block_rows),
        mask_piece,
    )
    result, unused = lax.scan(absorb, start_state, inputs)
    final_max, final_sum, weighted = result
    attended = (
        jnp.transpose(weighted / final_sum[:, :, None], (1, 0, 2))
        .reshape(row_count, head_cols)
        .astype(jnp.bfloat16)
    )
    branch = jnp.dot(attended, w_out, preferred_element_type=jnp.float32)
    after_attn = (placed.astype(jnp.float32) + branch).astype(jnp.bfloat16)
    conv_normed = layer_norm(after_attn, conv_gain).astype(jnp.bfloat16)
    channels = w_depth.shape[1]
    projected = jnp.dot(
        conv_normed,
        lax.all_gather(w_pointin, ("dp", "ctx"), axis=0, tiled=True),
        preferred_element_type=jnp.float32,
    )
    gated = (projected[:, :channels] * jax.nn.sigmoid(projected[:, channels:])).astype(jnp.bfloat16)
    kernel_len = w_depth.shape[0]
    half_len = kernel_len // 2
    padded = padded_2(gated, (("ctx", 0),), half_len)
    padded_f = padded.astype(jnp.float32)
    seg_pad = jnp.pad(seg_row, (half_len, half_len), constant_values=-1)
    seg_near = lax.dynamic_slice_in_dim(seg_pad, shard_start, row_count + 2 * half_len, 0)
    depthwise = jnp.zeros((row_count, channels), jnp.float32)
    for tap_index in range(kernel_len):
        same_seg = (seg_near[tap_index : tap_index + row_count] == own_seg).astype(jnp.float32)
        depthwise = (
            depthwise
            + w_depth[tap_index][None, :]
            * padded_f[tap_index : tap_index + row_count]
            * same_seg[:, None]
        )
    shifted = depthwise * bn_scale + bn_shift
    activated = (shifted * jax.nn.sigmoid(shifted)).astype(jnp.bfloat16)
    closing = jnp.dot(
        activated,
        lax.all_gather(w_pointout, ("dp", "ctx"), axis=1, tiled=True),
        preferred_element_type=jnp.float32,
    )
    layer_out = (after_attn.astype(jnp.float32) + closing).astype(jnp.bfloat16)
    return layer_out[None]


def solution(mesh):
    return jax.shard_map(
        per_device,
        mesh=mesh,
        in_specs=(
            P("dp", "ctx", None),
            P("dp", "ctx"),
            P("dp", None),
            P("dp", "ctx", None),
            P(),
            P(),
            P(),
            P(),
            P(("dp", "ctx"), None),
            P(None, ("dp", "ctx")),
            P(),
            P(),
            P(),
        ),
        out_specs=P("dp", "ctx", None),
        check_vma=False,
    )
```

profile of v0, /device:TPU:32, one launch (start us, length us, event | category | flops | bytes accessed | tf_op | source)
XLA Modules:
  0.0 1003.4 jit_solution(10388988709967639840)
XLA Ops:
  6.5 0.8 and_select_fusion.2
  7.4 0.6 reduce-window.6
  8.0 0.2 slice_reduce_fusion
  8.2 0.7 and_select_fusion.1
  8.9 0.1 fusion.115
  9.0 0.7 compare_select_fusion.1
  9.7 1.4 scatter_custom_fusion
  11.1 0.7 all_to_all.9
  11.8 14.2 %all-to-all-start = ((s32[64,1,8]{2,1,0:T(1,128)}), s32[64,1,8]{2,1,0:T(1,128)S(1)}, u32[]{:S(2)}, u32[]{:S(2)}) async-start(s32[64,1,8]{2,1,0:T(1,128)} %bitcast.6), calls=%async_computation | async-start | bytes 65536 | tf_op jit(solution)/shard_map/all_to_all | solution.py:76
  26.1 3.7 scatter_custom_fusion.1
  29.8 7.1 all-to-all-done
  36.9 6.3 all-to-all-start.1
  43.3 0.6 broadcast.383
  43.9 0.8 reduce.73
  44.6 0.1 reshape.284
  44.7 39.0 %all-to-all-done.1 = bf16[64,8,1536]{2,1,0:T(8,128)(2,1)} async-done(((bf16[64,8,1536]{2,1,0:T(8,128)(2,1)}), bf16[64,8,1536]{2,1,0:T(8,128)(2,1)}, u32[]{:S(2)}, u32[]{:S(2)}) %all-to-all-start.1) | async-done | bytes 1572896 | tf_op jit(solution)/shard_map/all_to_all | solution.py:69
  83.7 4.0 scatter_custom_fusion.2
  87.7 0.2 convert_reduce_fusion
  87.9 0.3 fusion.26
  88.3 5.1 convolution_convert_fusion
  93.4 0.9 fusion.120
  94.4 2.0 copy.31
  96.4 1.9 copy.29
  98.4 0.7 all-gather.11.cloned.1.call-update
  99.1 0.2 all-gather.13.cloned.1.call-start
  99.3 0.3 all-gather.13.cloned.1.call-update
  99.7 0.7 reduce.72
  100.4 0.1 pad_dynamic-slice_fusion
  100.5 0.7 compare_convert_fusion.31
  101.2 0.7 compare_convert_fusion.30
  101.9 0.1 reshape_squeeze.7
  102.0 0.2 slice_reduce_fusion.32
  102.1 0.2 copy.30
  102.3 15.2 %all-gather.9.cloned.1.call-done = bf16[1024,8,96]{0,2,1:T(8,128)(2,1)} async-done(((bf16[256,8,96]{0,2,1:T(8,128)(2,1)}), bf16[1024,8,96]{0,2,1:T(8,128)(2,1)}) %all-gather.9.cloned.1.call-update) | async-done | bytes 1572880 | tf_op jit(solution)/shard_map/all_gather | solution.py:127
  117.5 2.7 copy.43
  120.2 27.3 %all-gather.7.cloned.1.call-done = bf16[1024,8,96]{0,2,1:T(8,128)(2,1)} async-done(((bf16[256,8,96]{0,2,1:T(8,128)(2,1)}), bf16[1024,8,96]{0,2,1:T(8,128)(2,1)}) %all-gather.7.cloned.1.call-update) | async-done | bytes 1572880 | tf_op jit(solution)/shard_map/all_gather | solution.py:126
  147.5 2.7 copy.44
  150.3 22.4 %while.15 = (s32[]{:T(128)}, f32[8,256]{1,0:T(8,128)S(1)}, f32[8,256]{1,0:T(8,128)S(1)}, f32[8,256,96]{1,2,0:T(8,128)}, s32[256]{0:T(256)S(1)}, /*index=5*/s32[2...) while((s32[]{:T(128)}, f32[8,256]{1,0:T(8,128)S(1)}, ...), condition=%wide.region_11.12_spmd.clone, body=%wide.region_8.11_spmd.clone.sunk | while | flops 417146880 | bytes 33564948 | solution.py:141
  150.3 0.1 broadcast_bitcast_fusion.2
  150.4 0.2 bitcast_and_fusion.2
  150.6 4.1 fusion.139
  154.6 3.3 fusion.140
  158.0 0.1 copy-done.1
  158.1 3.3 fusion.142
  161.4 0.2 bitcast_and_fusion.2
  161.6 4.1 fusion.139
  165.7 3.4 fusion.140
  169.0 0.1 copy-done.1
  169.1 3.5 fusion.142
  172.7 1.3 divide_convert_fusion
  174.0 0.1 copy-done.3
  174.0 0.9 fusion.122
  174.9 1.1 copy-done.4
  176.1 0.3 multiply_reduce_fusion
  176.4 394.0 %all-gather.11.cloned.1.call-done = bf16[256,6,1536]{2,1,0:T(8,128)(2,1)} async-done(((bf16[1,6,1536]{2,1,0:T(8,128)(2,1)}), bf16[256,6,1536]{2,1,0:T(8,128)(2,1)}) %all-gather.11.cloned.1.call-update) | async-done | bytes 4718608 | tf_op jit(solution)/shard_map/all_gather | solution.py:154
  570.4 8.5 reshape.317
  578.8 4.3 fusion.31
  583.1 0.2 fusion.111
  583.3 1.3 collective-permute-start
  584.6 1.3 collective-permute-start.1
  585.9 0.1 slice_reduce_fusion.31
  586.3 396.1 %all-gather.13.cloned.1.call-done = bf16[256,6,768]{2,1,0:T(8,128)(2,1)} async-done(((bf16[1,6,768]{2,1,0:T(8,128)(2,1)}), bf16[256,6,768]{2,1,0:T(8,128)(2,1)}) %all-gather.13.cloned.1.call-update) | async-done | bytes 2359312 | tf_op jit(solution)/shard_map/all_gather | solution.py:177
  982.3 5.1 reshape.319
  987.7 9.2 fusion.23
  (91 shorter events, 0.6 us)
Async XLA Ops:
  6.5 167.4 %copy-start = (bf16[768,1536]{1,0:T(8,128)(2,1)S(1)}, bf16[768,1536]{1,0:T(8,128)(2,1)}, u32[]{:S(2)}) copy-start(bf16[768,1536]{1,0:T(8,128)(2,1)} %param.21) | copy-start | bytes 7077892
  11.8 25.1 %all-to-all-start = ((s32[64,1,8]{2,1,0:T(1,128)}), s32[64,1,8]{2,1,0:T(1,128)S(1)}, u32[]{:S(2)}, u32[]{:S(2)}) async-start(s32[64,1,8]{2,1,0:T(1,128)} %bitcast.6), calls=%async_computation | async-start | bytes 65536 | tf_op jit(solution)/shard_map/all_to_all | solution.py:76
  36.9 46.8 %all-to-all-start.1 = ((bf16[64,8,1536]{2,1,0:T(8,128)(2,1)}), bf16[64,8,1536]{2,1,0:T(8,128)(2,1)}, u32[]{:S(2)}, u32[]{:S(2)}) async-start(bf16[64,8,1536]{2,1,0:T(8,128)(2,1)} %bitcast.124), calls=%async_computation.1 | async-start | bytes 3145728 | tf_op jit(solution)/shard_map/all_to_all | solution.py:69
  43.2 74.3 %all-gather.9.cloned.1.call-start = ((), (), s32[]{:S(2)}) async-start(), calls=%async_computation.3 | async-start | bytes 1966080 | tf_op jit(solution)/shard_map/all_gather | solution.py:127
  83.7 4.5 copy-start.25
  87.7 5.7 copy-start.2
  94.4 5.3 copy-start.6
  94.4 7.5 copy-start.7
  94.4 7.6 copy-start.5
  96.4 51.2 %all-gather.7.cloned.1.call-start = ((), (), s32[]{:S(2)}) async-start(), calls=%async_computation.2 | async-start | bytes 1966080 | tf_op jit(solution)/shard_map/all_gather | solution.py:126
  98.4 472.0 %all-gather.11.cloned.1.call-start = ((), (), s32[]{:S(2)}) async-start(), calls=%async_computation.4 | async-start | bytes 6316032 | tf_op jit(solution)/shard_map/all_gather | solution.py:154
  99.1 883.2 %all-gather.13.cloned.1.call-start = ((), (), s32[]{:S(2)}) async-start(), calls=%async_computation.5 | async-start | bytes 3158016 | tf_op jit(solution)/shard_map/all_gather | solution.py:177
  154.6 3.4 copy-start.1
  165.7 3.5 copy-start.1
  172.7 1.4 copy-start.3
  174.9 1.1 copy-start.4
  176.4 402.5 %copy-start.26 = (f32[1536]{0:T(1024)S(1)}, f32[1536]{0:T(1024)}, u32[]{:S(2)}) copy-start(f32[1536]{0:T(1024)} %param.22) | copy-start | bytes 18436
  583.3 404.1 %collective-permute-start = (bf16[16,768]{1,0:T(8,128)(2,1)S(1)}, bf16[16,768]{1,0:T(8,128)(2,1)S(1)}, u32[]{:S(2)}, u32[]{:S(2)}) collective-permute-start(bf16[16,768]{1,0:T(8,128)(2,1)S(1)} %get-tuple-element.182), channel_id=1, source_target_pairs={{0,1},{1,2},{2,3},{4,5},{5,6},{6,7},{8,9},{9,10},{10,11},{12,13},{... | collective-permute-start | bytes 73736 | tf_op jit(solution)/shard_map/ppermute | solution.py:18
  584.6 402.8 %collective-permute-start.1 = (bf16[16,768]{1,0:T(8,128)(2,1)S(1)}, bf16[16,768]{1,0:T(8,128)(2,1)S(1)}, u32[]{:S(2)}, u32[]{:S(2)}) collective-permute-start(bf16[16,768]{1,0:T(8,128)(2,1)S(1)} %get-tuple-element.183), channel_id=1, source_target_pairs={{1,0},{2,1},{3,2},{5,4},{6,5},{7,6},{9,8},{10,9},{11,10},{13,12},{... | collective-permute-start | bytes 73736 | tf_op jit(solution)/shard_map/ppermute | solution.py:20
  586.1 401.4 %copy-start.8 = (f32[256]{0:T(256)S(1)}, f32[256]{0:T(256)}, u32[]{:S(2)}) copy-start(f32[256]{0:T(256)} %get-tuple-element.199) | copy-start | bytes 3076
  586.1 401.4 %copy-start.9 = (f32[256]{0:T(256)S(1)}, f32[256]{0:T(256)}, u32[]{:S(2)}) copy-start(f32[256]{0:T(256)} %get-tuple-element.200) | copy-start | bytes 3076
  586.1 401.4 %copy-start.10 = (f32[256]{0:T(256)S(1)}, f32[256]{0:T(256)}, u32[]{:S(2)}) copy-start(f32[256]{0:T(256)} %get-tuple-element.201) | copy-start | bytes 3076
  586.1 401.4 %copy-start.11 = (f32[256]{0:T(256)S(1)}, f32[256]{0:T(256)}, u32[]{:S(2)}) copy-start(f32[256]{0:T(256)} %get-tuple-element.202) | copy-start | bytes 3076
  586.1 401.4 %copy-start.12 = (f32[256]{0:T(256)S(1)}, f32[256]{0:T(256)}, u32[]{:S(2)}) copy-start(f32[256]{0:T(256)} %get-tuple-element.203) | copy-start | bytes 3076
  586.1 401.4 %copy-start.13 = (f32[256]{0:T(256)S(1)}, f32[256]{0:T(256)}, u32[]{:S(2)}) copy-start(f32[256]{0:T(256)} %get-tuple-element.204) | copy-start | bytes 3076
  586.1 401.4 %copy-start.14 = (f32[256]{0:T(256)S(1)}, f32[256]{0:T(256)}, u32[]{:S(2)}) copy-start(f32[256]{0:T(256)} %get-tuple-element.205) | copy-start | bytes 3076
  586.1 401.4 %copy-start.15 = (f32[256]{0:T(256)S(1)}, f32[256]{0:T(256)}, u32[]{:S(2)}) copy-start(f32[256]{0:T(256)} %get-tuple-element.206) | copy-start | bytes 3076
  586.1 401.4 %copy-start.16 = (f32[256]{0:T(256)S(1)}, f32[256]{0:T(256)}, u32[]{:S(2)}) copy-start(f32[256]{0:T(256)} %get-tuple-element.207) | copy-start | bytes 3076
  586.1 401.4 %copy-start.17 = (f32[256]{0:T(256)S(1)}, f32[256]{0:T(256)}, u32[]{:S(2)}) copy-start(f32[256]{0:T(256)} %get-tuple-element.208) | copy-start | bytes 3076
  586.2 401.4 %copy-start.18 = (f32[256]{0:T(256)S(1)}, f32[256]{0:T(256)}, u32[]{:S(2)}) copy-start(f32[256]{0:T(256)} %get-tuple-element.209) | copy-start | bytes 3076
  586.2 401.4 %copy-start.19 = (f32[256]{0:T(256)S(1)}, f32[256]{0:T(256)}, u32[]{:S(2)}) copy-start(f32[256]{0:T(256)} %get-tuple-element.210) | copy-start | bytes 3076
  586.2 401.4 %copy-start.20 = (f32[256]{0:T(256)S(1)}, f32[256]{0:T(256)}, u32[]{:S(2)}) copy-start(f32[256]{0:T(256)} %get-tuple-element.211) | copy-start | bytes 3076
  586.2 401.4 %copy-start.21 = (f32[256]{0:T(256)S(1)}, f32[256]{0:T(256)}, u32[]{:S(2)}) copy-start(f32[256]{0:T(256)} %get-tuple-element.212) | copy-start | bytes 3076
  586.2 401.4 %copy-start.22 = (f32[256]{0:T(256)S(1)}, f32[256]{0:T(256)}, u32[]{:S(2)}) copy-start(f32[256]{0:T(256)} %get-tuple-element.213) | copy-start | bytes 3076
  586.2 401.4 %copy-start.23 = (f32[256]{0:T(256)S(1)}, f32[256]{0:T(256)}, u32[]{:S(2)}) copy-start(f32[256]{0:T(256)} %get-tuple-element.214) | copy-start | bytes 3076
  586.2 401.4 %copy-start.24 = (f32[256]{0:T(256)S(1)}, f32[256]{0:T(256)}, u32[]{:S(2)}) copy-start(f32[256]{0:T(256)} %get-tuple-element.215) | copy-start | bytes 3076
  586.2 401.4 %copy-start.27 = (f32[768]{0:T(1024)S(1)}, f32[768]{0:T(1024)}, u32[]{:S(2)}) copy-start(f32[768]{0:T(1024)} %param.27) | copy-start | bytes 9220
  586.2 401.4 %copy-start.28 = (f32[768]{0:T(1024)S(1)}, f32[768]{0:T(1024)}, u32[]{:S(2)}) copy-start(f32[768]{0:T(1024)} %param.26) | copy-start | bytes 9220
Sparse Core Ops, SparseCore 0:
  96.5 20.9 all-gather.8
  119.3 28.2 all-gather.6
  149.4 420.8 all-gather.10
  572.1 410.1 all-gather.12
where the time goes:
time: 1000 us
  waiting for transfers between devices  880 us (88%)
  local copies, waits for them, and re-layouts  36.8 us (4%)
  matrix products  34.4 us (3%)
  starting transfers between devices  23.4 us (2%)
  other arithmetic  15.3 us (2%)
  between operations  13.7 us (1%)
    all_gather x1, waiting for transfers between devices, per_device(): lax.all_gather(w_pointout, ('dp', 'ctx'), axis=1, tiled=True)  396 us
    all_gather x1, waiting for transfers between devices, per_device(): lax.all_gather(w_pointin, ('dp', 'ctx'), axis=0, tiled=True)  394 us
    all_to_all x1, waiting for transfers between devices, per_device(): lax.all_to_all(send_rows.reshape(peer_count, capacity, width), 'dp', spli...  39 us
    all_gather x1, waiting for transfers between devices, per_device(): keys_piece = lax.all_gather(key_rows, 'ctx', axis=0, tiled=True)  27.3 us
  transfers between devices with their start and end apart: 8, of which 6 were waited for; matrix products, arithmetic and copies ran while one was open for 6% of the time, Pallas kernels for 0%

commit v1 on v0

--- a/solution.py
+++ b/solution.py
@@ -151,7 +151,12 @@
     channels = w_depth.shape[1]
     projected = jnp.dot(
         conv_normed,
-        lax.all_gather(w_pointin, ("dp", "ctx"), axis=0, tiled=True),
+        jnp.concatenate(
+            lax.all_to_all(
+                jnp.stack([w_pointin] * lax.axis_size(("dp", "ctx"))), ("dp", "ctx"), 0, 0
+            ),
+            axis=0,
+        ),
         preferred_element_type=jnp.float32,
     )
     gated = (projected[:, :channels] * jax.nn.sigmoid(projected[:, channels:])).astype(jnp.bfloat16)

time: 1000 us -> 637 us (0.64); the launches traced: 1000 us -> 627 us
  waiting for transfers between devices: 880 us -> 493 us
    all_gather x1 -> x0, waiting for transfers between devices: 394 us -> none  [per_device(): lax.all_gather(w_pointin, ('dp', 'ctx'), axis=0, tiled=True)]
    all_gather x1, waiting for transfers between devices: 396 us -> 341 us  [per_device(): lax.all_gather(w_pointout, ('dp', 'ctx'), axis=1, tiled=True)]
    all_to_all x0 -> x1, waiting for transfers between devices: none -> 38.7 us  [per_device(): lax.all_to_all(jnp.stack([w_pointin] * lax.axis_size(('dp', 'ctx'))), ('d...]
    all_gather x1, waiting for transfers between devices: 27.3 us -> 40.2 us  [per_device(): keys_piece = lax.all_gather(key_rows, 'ctx', axis=0, tiled=True)]
    all_gather x1, waiting for transfers between devices: 15.2 us -> 26.4 us  [per_device(): values_piece = lax.all_gather(value_rows, 'ctx', axis=0, tiled=True)]
  transfers between devices with their start and end apart: 8 -> 8, of which waited for: 6 -> 6; matrix products, arithmetic and copies ran while one was open for 6% -> 10% of each run, Pallas kernels for 0% -> 0%
where the time goes in v1:
time: 637 us; the launch traced here: 627 us
  waiting for transfers between devices  493 us (77%)
  local copies, waits for them, and re-layouts  39.6 us (6%)
  matrix products  34.2 us (5%)
  starting transfers between devices  31.2 us (5%)
  other arithmetic  15 us (2%)
  between operations  13.7 us (2%)
    all_gather x1, waiting for transfers between devices, per_device(): lax.all_gather(w_pointout, ('dp', 'ctx'), axis=1, tiled=True)  341 us
    all_gather x1, waiting for transfers between devices, per_device(): keys_piece = lax.all_gather(key_rows, 'ctx', axis=0, tiled=True)  40.2 us
    all_to_all x1, waiting for transfers between devices, per_device(): lax.all_to_all(send_rows.reshape(peer_count, capacity, width), 'dp', spli...  39.3 us
    all_to_all x1, waiting for transfers between devices, per_device(): lax.all_to_all(jnp.stack([w_pointin] * lax.axis_size(('dp', 'ctx'))), ('d...  38.7 us
    all_gather x1, waiting for transfers between devices, per_device(): values_piece = lax.all_gather(value_rows, 'ctx', axis=0, tiled=True)  26.4 us
    all_to_all x1, starting transfers between devices, per_device(): lax.all_to_all(send_slots.reshape(peer_count, capacity), 'dp', split_axis...  14.2 us
  transfers between devices with their start and end apart: 8, of which 6 were waited for; matrix products, arithmetic and copies ran while one was open for 10% of the time, Pallas kernels for 0%

profile of v1, /device:TPU:32, one launch (start us, length us, event | category | flops | bytes accessed | tf_op | source)
XLA Modules:
  0.0 627.1 jit_solution(23702905049726879)
XLA Ops:
  6.5 0.8 and_select_fusion.2
  7.4 0.6 reduce-window.6
  8.0 0.2 slice_reduce_fusion
  8.2 0.7 and_select_fusion.1
  8.9 0.1 fusion.115
  9.0 0.7 compare_select_fusion.1
  9.7 1.4 scatter_custom_fusion
  11.1 0.7 all_to_all.12
  11.8 14.2 %all-to-all-start = ((s32[64,1,8]{2,1,0:T(1,128)}), s32[64,1,8]{2,1,0:T(1,128)S(1)}, u32[]{:S(2)}, u32[]{:S(2)}) async-start(s32[64,1,8]{2,1,0:T(1,128)} %bitcast.6), calls=%async_computation | async-start | bytes 65536 | tf_op jit(solution)/shard_map/all_to_all | solution.py:76
  26.1 3.7 scatter_custom_fusion.1
  29.8 7.1 %all-to-all-done = s32[64,1,8]{2,1,0:T(1,128)S(1)} async-done(((s32[64,1,8]{2,1,0:T(1,128)}), s32[64,1,8]{2,1,0:T(1,128)S(1)}, u32[]{:S(2)}, u32[]{:S(2)}) %all-to-all-start) | async-done | bytes 2080 | tf_op jit(solution)/shard_map/all_to_all | solution.py:76
  36.9 6.3 %all-to-all-start.1 = ((bf16[64,8,1536]{2,1,0:T(8,128)(2,1)}), bf16[64,8,1536]{2,1,0:T(8,128)(2,1)}, u32[]{:S(2)}, u32[]{:S(2)}) async-start(bf16[64,8,1536]{2,1,0:T(8,128)(2,1)} %bitcast.123), calls=%async_computation.1 | async-start | bytes 3145728 | tf_op jit(solution)/shard_map/all_to_all | solution.py:69
  43.3 0.5 broadcast.385
  43.7 0.6 reduce.73
  44.4 0.1 reshape.289
  44.5 39.3 %all-to-all-done.1 = bf16[64,8,1536]{2,1,0:T(8,128)(2,1)} async-done(((bf16[64,8,1536]{2,1,0:T(8,128)(2,1)}), bf16[64,8,1536]{2,1,0:T(8,128)(2,1)}, u32[]{:S(2)}, u32[]{:S(2)}) %all-to-all-start.1) | async-done | bytes 1572896 | tf_op jit(solution)/shard_map/all_to_all | solution.py:69
  83.7 4.0 scatter_custom_fusion.2
  87.7 0.2 convert_reduce_fusion
  87.9 0.3 fusion.26
  88.3 5.1 convolution_convert_fusion
  93.4 1.0 fusion.120
  94.4 1.9 copy.31
  96.3 3.8 stack.2
  100.1 7.3 %all-to-all-start.2 = ((bf16[256,6,1536]{2,1,0:T(8,128)(2,1)}), bf16[256,6,1536]{2,1,0:T(8,128)(2,1)}, u32[]{:S(2)}, u32[]{:S(2)}) async-start(bf16[256,6,1536]{2,1,0:T(8,128)(2,1)} %stack.2), calls=%async_computation.2 | async-start | bytes 12582912 | tf_op jit(solution)/shard_map/all_to_all | solution.py:155
  107.5 0.9 copy.29
  108.5 0.7 all-gather.9.cloned.1.call-update
  109.2 0.6 reduce.72
  109.8 0.1 reshape_squeeze.7
  109.9 0.1 pad_dynamic-slice_fusion
  110.0 0.2 slice_reduce_fusion.32
  110.1 0.7 compare_convert_fusion.30
  110.9 0.6 compare_convert_fusion.31
  111.5 0.2 copy.30
  111.6 26.4 %all-gather.7.cloned.1.call-done = bf16[1024,8,96]{0,2,1:T(8,128)(2,1)} async-done(((bf16[256,8,96]{0,2,1:T(8,128)(2,1)}), bf16[1024,8,96]{0,2,1:T(8,128)(2,1)}) %all-gather.7.cloned.1.call-update) | async-done | bytes 1572880 | tf_op jit(solution)/shard_map/all_gather | solution.py:127
  138.0 2.7 copy.43
  140.8 40.2 %all-gather.5.cloned.1.call-done = bf16[1024,8,96]{0,2,1:T(8,128)(2,1)} async-done(((bf16[256,8,96]{0,2,1:T(8,128)(2,1)}), bf16[1024,8,96]{0,2,1:T(8,128)(2,1)}) %all-gather.5.cloned.1.call-update) | async-done | bytes 1572880 | tf_op jit(solution)/shard_map/all_gather | solution.py:126
  181.0 2.8 copy.44
  183.7 22.2 %while.15 = (s32[]{:T(128)}, f32[8,256]{1,0:T(8,128)S(1)}, f32[8,256]{1,0:T(8,128)S(1)}, f32[8,256,96]{1,2,0:T(8,128)}, s32[256]{0:T(256)S(1)}, /*index=5*/s32[2...) while((s32[]{:T(128)}, f32[8,256]{1,0:T(8,128)S(1)}, ...), condition=%wide.region_11.12_spmd.clone, body=%wide.region_8.11_spmd.clone.sunk | while | flops 417146880 | bytes 33564948 | solution.py:141
  183.7 0.1 broadcast_bitcast_fusion.2
  183.8 0.2 bitcast_and_fusion.2
  184.0 4.0 fusion.139
  188.0 3.3 fusion.140
  191.3 0.1 copy-done.1
  191.4 3.3 fusion.142
  194.8 0.2 bitcast_and_fusion.2
  195.0 4.0 fusion.139
  199.0 3.3 fusion.140
  202.3 0.1 copy-done.1
  202.4 3.5 fusion.142
  205.9 1.3 divide_convert_fusion
  207.2 0.1 copy-done.3
  207.3 0.9 fusion.122
  208.2 1.2 copy-done.4
  209.4 0.3 multiply_reduce_fusion
  209.7 38.7 %all-to-all-done.2 = bf16[256,6,1536]{2,1,0:T(8,128)(2,1)} async-done(((bf16[256,6,1536]{2,1,0:T(8,128)(2,1)}), bf16[256,6,1536]{2,1,0:T(8,128)(2,1)}, u32[]{:S(2)}, u32[]{:S(2)}) %all-to-all-start.2) | async-done | bytes 4718624 | tf_op jit(solution)/shard_map/all_to_all | solution.py:155
  248.4 8.5 %reshape.297 = bf16[1536,1536]{1,0:T(8,128)(2,1)} reshape(bf16[256,6,1536]{2,1,0:T(8,128)(2,1)} %all-to-all-done.2) | data formatting | bytes 9437184 | tf_op jit(solution)/shard_map/reshape | solution.py:154
  256.9 4.3 fusion.31
  261.1 0.2 fusion.111
  261.4 2.0 collective-permute-start
  263.4 1.3 collective-permute-start.1
  264.7 0.1 slice_reduce_fusion.31
  265.0 341.0 %all-gather.9.cloned.1.call-done = bf16[256,6,768]{2,1,0:T(8,128)(2,1)} async-done(((bf16[1,6,768]{2,1,0:T(8,128)(2,1)}), bf16[256,6,768]{2,1,0:T(8,128)(2,1)}) %all-gather.9.cloned.1.call-update) | async-done | bytes 2359312 | tf_op jit(solution)/shard_map/all_gather | solution.py:182
  606.0 5.1 reshape.323
  611.3 9.2 %fusion.23 = bf16[1,256,1536]{2,1,0:T(8,128)(2,1)} fusion(f32[256,1536]{1,0:T(8,128)} %copy-done.4, bf16[1536,768]{1,0:T(8,128)(2,1)} %reshape.323, f32[288,768]{1,0:T(8,128)S(1)} %maximum_convert_fusion, f32[768]{0:T(1024)S(1)} %copy-done.28, f32[768]{0:T(1024)S(1)} %copy-done.29, f32[256]{0:T(256)S(1)} %get-tuple-element.185, ...), kind=kOutput, calls=%fused_computation.37 | convolution fusion | flops 624820224 | bytes 30056448 | tf_op jit(solution)/shard_map/dot_general | solution.py:180
  (93 shorter events, 0.6 us)
Async XLA Ops:
  6.5 200.7 %copy-start = (bf16[768,1536]{1,0:T(8,128)(2,1)S(1)}, bf16[768,1536]{1,0:T(8,128)(2,1)}, u32[]{:S(2)}) copy-start(bf16[768,1536]{1,0:T(8,128)(2,1)} %param.21) | copy-start | bytes 7077892
  11.8 25.1 %all-to-all-start = ((s32[64,1,8]{2,1,0:T(1,128)}), s32[64,1,8]{2,1,0:T(1,128)S(1)}, u32[]{:S(2)}, u32[]{:S(2)}) async-start(s32[64,1,8]{2,1,0:T(1,128)} %bitcast.6), calls=%async_computation | async-start | bytes 65536 | tf_op jit(solution)/shard_map/all_to_all | solution.py:76
  36.9 46.8 %all-to-all-start.1 = ((bf16[64,8,1536]{2,1,0:T(8,128)(2,1)}), bf16[64,8,1536]{2,1,0:T(8,128)(2,1)}, u32[]{:S(2)}, u32[]{:S(2)}) async-start(bf16[64,8,1536]{2,1,0:T(8,128)(2,1)} %bitcast.123), calls=%async_computation.1 | async-start | bytes 3145728 | tf_op jit(solution)/shard_map/all_to_all | solution.py:69
  43.2 94.8 %all-gather.7.cloned.1.call-start = ((), (), s32[]{:S(2)}) async-start(), calls=%async_computation.4 | async-start | bytes 1966080 | tf_op jit(solution)/shard_map/all_gather | solution.py:127
  83.7 4.5 copy-start.26
  87.7 5.7 copy-start.2
  100.1 7.3 %copy-start.5 = (bf16[256,768]{1,0:T(8,128)(2,1)S(1)}, bf16[256,768]{1,0:T(8,128)(2,1)}, u32[]{:S(2)}) copy-start(bf16[256,768]{1,0:T(8,128)(2,1)} %get-tuple-element.181) | copy-start | bytes 1179652
  100.1 9.1 %copy-start.7 = (s32[1,1024]{1,0:T(1,128)S(1)}, s32[1,1024]{1,0:T(1,128)}, u32[]{:S(2)}) copy-start(s32[1,1024]{1,0:T(1,128)} %param.17) | copy-start | bytes 12292
  100.1 9.7 %copy-start.8 = (s32[1,2,8]{2,1,0:T(2,128)S(1)}, s32[1,2,8]{2,1,0:T(2,128)}, u32[]{:S(2)}) copy-start(s32[1,2,8]{2,1,0:T(2,128)} %param.18) | copy-start | bytes 196
  100.1 9.8 %copy-start.6 = (f32[32,768]{1,0:T(8,128)S(1)}, f32[32,768]{1,0:T(8,128)}, u32[]{:S(2)}) copy-start(f32[32,768]{1,0:T(8,128)} %param.25) | copy-start | bytes 294916
  100.1 148.3 %all-to-all-start.2 = ((bf16[256,6,1536]{2,1,0:T(8,128)(2,1)}), bf16[256,6,1536]{2,1,0:T(8,128)(2,1)}, u32[]{:S(2)}, u32[]{:S(2)}) async-start(bf16[256,6,1536]{2,1,0:T(8,128)(2,1)} %stack.2), calls=%async_computation.2 | async-start | bytes 12582912 | tf_op jit(solution)/shard_map/all_to_all | solution.py:155
  107.4 73.5 %all-gather.5.cloned.1.call-start = ((), (), s32[]{:S(2)}) async-start(), calls=%async_computation.3 | async-start | bytes 1966080 | tf_op jit(solution)/shard_map/all_gather | solution.py:126
  108.4 497.5 %all-gather.9.cloned.1.call-start = ((), (), s32[]{:S(2)}) async-start(), calls=%async_computation.5 | async-start | bytes 3158016 | tf_op jit(solution)/shard_map/all_gather | solution.py:182
  188.0 3.4 copy-start.1
  199.0 3.4 copy-start.1
  205.9 1.4 copy-start.3
  208.2 1.2 copy-start.4
  209.7 47.2 %copy-start.27 = (f32[1536]{0:T(1024)S(1)}, f32[1536]{0:T(1024)}, u32[]{:S(2)}) copy-start(f32[1536]{0:T(1024)} %param.22) | copy-start | bytes 18436
  261.4 349.7 %collective-permute-start = (bf16[16,768]{1,0:T(8,128)(2,1)S(1)}, bf16[16,768]{1,0:T(8,128)(2,1)S(1)}, u32[]{:S(2)}, u32[]{:S(2)}) collective-permute-start(bf16[16,768]{1,0:T(8,128)(2,1)S(1)} %get-tuple-element.182), channel_id=1, source_target_pairs={{0,1},{1,2},{2,3},{4,5},{5,6},{6,7},{8,9},{9,10},{10,11},{12,13},{... | collective-permute-start | bytes 73736 | tf_op jit(solution)/shard_map/ppermute | solution.py:18
  263.4 347.7 %collective-permute-start.1 = (bf16[16,768]{1,0:T(8,128)(2,1)S(1)}, bf16[16,768]{1,0:T(8,128)(2,1)S(1)}, u32[]{:S(2)}, u32[]{:S(2)}) collective-permute-start(bf16[16,768]{1,0:T(8,128)(2,1)S(1)} %get-tuple-element.183), channel_id=1, source_target_pairs={{1,0},{2,1},{3,2},{5,4},{6,5},{7,6},{9,8},{10,9},{11,10},{13,12},{... | collective-permute-start | bytes 73736 | tf_op jit(solution)/shard_map/ppermute | solution.py:20
  264.8 346.4 %copy-start.9 = (f32[256]{0:T(256)S(1)}, f32[256]{0:T(256)}, u32[]{:S(2)}) copy-start(f32[256]{0:T(256)} %get-tuple-element.199) | copy-start | bytes 3076
  264.8 346.4 %copy-start.10 = (f32[256]{0:T(256)S(1)}, f32[256]{0:T(256)}, u32[]{:S(2)}) copy-start(f32[256]{0:T(256)} %get-tuple-element.200) | copy-start | bytes 3076
  264.8 346.4 %copy-start.11 = (f32[256]{0:T(256)S(1)}, f32[256]{0:T(256)}, u32[]{:S(2)}) copy-start(f32[256]{0:T(256)} %get-tuple-element.201) | copy-start | bytes 3076
  264.8 346.4 %copy-start.12 = (f32[256]{0:T(256)S(1)}, f32[256]{0:T(256)}, u32[]{:S(2)}) copy-start(f32[256]{0:T(256)} %get-tuple-element.202) | copy-start | bytes 3076
  264.8 346.4 %copy-start.13 = (f32[256]{0:T(256)S(1)}, f32[256]{0:T(256)}, u32[]{:S(2)}) copy-start(f32[256]{0:T(256)} %get-tuple-element.203) | copy-start | bytes 3076
  264.8 346.4 %copy-start.14 = (f32[256]{0:T(256)S(1)}, f32[256]{0:T(256)}, u32[]{:S(2)}) copy-start(f32[256]{0:T(256)} %get-tuple-element.204) | copy-start | bytes 3076
  264.9 346.4 %copy-start.15 = (f32[256]{0:T(256)S(1)}, f32[256]{0:T(256)}, u32[]{:S(2)}) copy-start(f32[256]{0:T(256)} %get-tuple-element.205) | copy-start | bytes 3076
  264.9 346.4 %copy-start.16 = (f32[256]{0:T(256)S(1)}, f32[256]{0:T(256)}, u32[]{:S(2)}) copy-start(f32[256]{0:T(256)} %get-tuple-element.206) | copy-start | bytes 3076
  264.9 346.4 %copy-start.17 = (f32[256]{0:T(256)S(1)}, f32[256]{0:T(256)}, u32[]{:S(2)}) copy-start(f32[256]{0:T(256)} %get-tuple-element.207) | copy-start | bytes 3076
  264.9 346.4 %copy-start.18 = (f32[256]{0:T(256)S(1)}, f32[256]{0:T(256)}, u32[]{:S(2)}) copy-start(f32[256]{0:T(256)} %get-tuple-element.208) | copy-start | bytes 3076
  264.9 346.4 %copy-start.19 = (f32[256]{0:T(256)S(1)}, f32[256]{0:T(256)}, u32[]{:S(2)}) copy-start(f32[256]{0:T(256)} %get-tuple-element.209) | copy-start | bytes 3076
  264.9 346.4 %copy-start.20 = (f32[256]{0:T(256)S(1)}, f32[256]{0:T(256)}, u32[]{:S(2)}) copy-start(f32[256]{0:T(256)} %get-tuple-element.210) | copy-start | bytes 3076
  264.9 346.4 %copy-start.21 = (f32[256]{0:T(256)S(1)}, f32[256]{0:T(256)}, u32[]{:S(2)}) copy-start(f32[256]{0:T(256)} %get-tuple-element.211) | copy-start | bytes 3076
  264.9 346.4 %copy-start.22 = (f32[256]{0:T(256)S(1)}, f32[256]{0:T(256)}, u32[]{:S(2)}) copy-start(f32[256]{0:T(256)} %get-tuple-element.212) | copy-start | bytes 3076
  264.9 346.4 %copy-start.23 = (f32[256]{0:T(256)S(1)}, f32[256]{0:T(256)}, u32[]{:S(2)}) copy-start(f32[256]{0:T(256)} %get-tuple-element.213) | copy-start | bytes 3076
  264.9 346.4 %copy-start.24 = (f32[256]{0:T(256)S(1)}, f32[256]{0:T(256)}, u32[]{:S(2)}) copy-start(f32[256]{0:T(256)} %get-tuple-element.214) | copy-start | bytes 3076
  265.0 346.4 %copy-start.25 = (f32[256]{0:T(256)S(1)}, f32[256]{0:T(256)}, u32[]{:S(2)}) copy-start(f32[256]{0:T(256)} %get-tuple-element.215) | copy-start | bytes 3076
  265.0 346.4 %copy-start.28 = (f32[768]{0:T(1024)S(1)}, f32[768]{0:T(1024)}, u32[]{:S(2)}) copy-start(f32[768]{0:T(1024)} %param.27) | copy-start | bytes 9220
  265.0 346.4 %copy-start.29 = (f32[768]{0:T(1024)S(1)}, f32[768]{0:T(1024)}, u32[]{:S(2)}) copy-start(f32[768]{0:T(1024)} %param.26) | copy-start | bytes 9220
Sparse Core Ops, SparseCore 0:
  96.5 41.5 all-gather.6
  139.8 41.0 all-gather.4
  182.9 423.0 all-gather.8
